TPU v7x, 1024 devices: a whole 4x8x16 slice. The times are simulated.
1024 devices in a mesh: group: 4 (over x), ingroup: 32 (over z, core), cuts: 8 (over y).
Axes of the slice: x: 4, y: 8, z: 16, core: 2. Of those that a mesh axis runs over, the one named last changes fastest.
Arguments:
- tokens_q: bfloat16 [4096, 4096], P(('group', 'ingroup'), 'cuts'), may hold values from -6 to 6
- scale_exp: int32 [4096, 32], P(('group', 'ingroup'), 'cuts'), may hold values from -2 to 2
- routes: int32 [4096, 8], P(('group', 'ingroup')), may hold values from 0 to 127, all different within a row; in each aligned block of 32 rows (0 to 31, 32 to 63, ...) at most 4 rows name the same one
- route_scores: float32 [4096, 8], P(('group', 'ingroup')), may hold values from 0.05 to 1
- w_gate: bfloat16 [128, 4096, 1024], P(('group', 'ingroup'), 'cuts'), may hold values from -0.09375 to 0.09375
- w_up: bfloat16 [128, 4096, 1024], P(('group', 'ingroup'), 'cuts'), may hold values from -0.09375 to 0.09375
- w_down: bfloat16 [128, 1024, 4096], P(('group', 'ingroup'), None, 'cuts'), may hold values from -0.1875 to 0.1875
Outputs:
- mixed: bfloat16 [4096, 4096], P(('group', 'ingroup'), 'cuts')
Inputs may be any that keep to these rules, and one draw needn't show every extreme that they name: `routes`: each row names 8 different experts. In each aligned block of 32 rows (the rows of one index of group and ingroup) no expert is named by more than 4 rows, and in some block an expert is named by exactly 4.
All inputs are finite; a program needn't handle non-finite values.
Results may differ from a plain program's by a relative error of at most 0.029.
Values may be sent and summed in bfloat16 or wider, within the bound.
No kernel may reach another device: no remote copies, remote signals or barrier semaphores. Data moves between devices by JAX's collectives and lax.ppermute only.
A program may use at most 32 MiB of HBM per device.

v0:
```python
import jax
import jax.numpy as jnp
from jax import lax
from jax.experimental import pallas as pl
from jax.experimental.pallas import tpu as pltpu
from jax.sharding import Mesh, PartitionSpec as P

CAP = 4
LANES = 128
BF = jnp.bfloat16
F32 = jnp.float32
CHIPS = ("x", "z")


def message_kernel(tokens_ref, exp_ref, routes_ref, scores_ref, out_ref):
    tok, feat = tokens_ref.shape
    topk, blocks = routes_ref.shape[0], exp_ref.shape[0]
    factor = (1 << (exp_ref[...] + 16)).astype(F32) * (1.0 / 65536.0)
    scores = scores_ref[...]
    mix = 2.5 * scores / jnp.sum(scores, axis=0, keepdims=True)
    pad = jnp.zeros((LANES - 2 * topk - blocks, tok), F32)
    lines = jnp.concatenate([routes_ref[...].astype(F32), mix, factor, pad], axis=0).astype(BF)
    place = jax.lax.broadcasted_iota(jnp.int32, (LANES, LANES), 0)
    same = (place == jax.lax.broadcasted_iota(jnp.int32, (LANES, LANES), 1)).astype(BF)
    columns = lax.dot_general(lines, same, (((0,), (0,)), ((), ())), preferred_element_type=F32)
    for i in range(blocks):
        part = slice(i * LANES, (i + 1) * LANES)
        scale = columns[:, 2 * topk + i : 2 * topk + i + 1]
        out_ref[:, part] = (tokens_ref[:, part].astype(F32) * scale).astype(BF)
    out_ref[:, feat:] = columns.astype(BF)


def make_message(tokens_q, scale_exp, routes, route_scores):
    tok, feat = tokens_q.shape
    return pl.pallas_call(
        message_kernel,
        out_shape=jax.ShapeDtypeStruct((tok, feat + LANES), BF),
    )(tokens_q, scale_exp.T, routes.T, route_scores.T)


def along(value, step):
    size = lax.axis_size("y")
    return lax.ppermute(value, "y", [(i, (i + step) % size) for i in range(size)])


def exchange(value, axis):
    return lax.all_to_all(value, axis, split_axis=0, concat_axis=0, tiled=True)


def ring_sum(chunk_of, extra):
    size = lax.axis_size("y")
    right, left = size // 2, (size - 1) // 2
    width = chunk_of(0).shape[1]

    def join(k, arrived, block):
        part = chunk_of(k)
        if arrived is not None:
            part = part + arrived[:, :width].astype(F32)
        return jnp.concatenate([part.astype(BF), block], axis=1)

    total = extra.astype(F32)
    to_right = join(right, None, extra) if right else None
    to_left = join(-left, None, extra) if left else None
    for step in range(right):
        to_right = along(to_right, 1)
        if step < left:
            to_left = along(to_left, -1)
        total = total + to_right[:, width:].astype(F32)
        if step < left:
            total = total + to_left[:, width:].astype(F32)
        if step < right - 1:
            to_right = join(right - 1 - step, to_right, to_right[:, width:])
        if step < left - 1:
            to_left = join(step + 1 - left, to_left, to_left[:, width:])
    own = chunk_of(0)
    if right:
        own = own + to_right[:, :width].astype(F32)
    if left:
        own = own + to_left[:, :width].astype(F32)
    return own, total


def gated(gate, up):
    return (jax.nn.silu(gate) * up).astype(BF)


def per_device(tokens_q, scale_exp, routes, route_scores, w_gate, w_up, w_down):
    n_c, n_y, peers = lax.axis_size("c"), lax.axis_size("y"), lax.axis_size(CHIPS)
    tok, feat = tokens_q.shape
    topk = routes.shape[1]
    hid = w_gate.shape[2]
    tail_cols = LANES // (2 * n_y)
    core = lax.axis_index("c")
    y = lax.axis_index("y")
    slots = n_c * CAP
    total_rows = peers * slots

    message = make_message(tokens_q, scale_exp, routes, route_scores)
    pair = lax.all_gather(message, "c", axis=0, tiled=True)
    pair_routes = pair[:, feat : feat + topk].astype(jnp.int32)
    pair_mix = pair[:, feat + topk : feat + 2 * topk].astype(F32)

    expert = jnp.arange(peers, dtype=jnp.int32) * n_c + core
    picked = pair_routes[:, :, None] == expert[None, None, :]
    weight = jnp.sum(jnp.where(picked, pair_mix[:, :, None], 0.0), axis=1)
    named = jnp.any(picked, axis=1).astype(jnp.int32).reshape(n_c, tok, peers)
    before = jnp.cumsum(named, axis=1, dtype=jnp.int32) - named
    block = jnp.arange(n_c, dtype=jnp.int32)[:, None, None]
    slot = jnp.where(named > 0, block * CAP + before, -1).reshape(n_c * tok, peers)
    slot_ids = jnp.arange(slots, dtype=jnp.int32)
    select = slot.T[:, None, :] == slot_ids[None, :, None]
    select_rows = select.astype(BF).reshape(total_rows, n_c * tok)
    combine = jnp.where(select, weight.T[:, None, :], 0.0).astype(BF).reshape(total_rows, n_c * tok)

    packed = jnp.dot(select_rows, pair[:, :feat], preferred_element_type=F32).astype(BF)
    arrived = exchange(packed.reshape(peers, slots, feat), CHIPS).reshape(total_rows, feat)

    gate_part = jnp.dot(arrived, w_gate[0], preferred_element_type=F32).astype(BF)
    up_part = jnp.dot(arrived, w_up[0], preferred_element_type=F32).astype(BF)
    main = hid - tail_cols
    w_tail = jnp.concatenate([w_gate[0, :, main:], w_up[0, :, main:]], axis=1)
    tail_part = lax.dot_general(w_tail, arrived, (((0,), (1,)), ((), ())), preferred_element_type=F32).astype(BF)
    stacks = total_rows // LANES
    tail_part = tail_part.reshape(2 * tail_cols, stacks, LANES).transpose(1, 0, 2).reshape(stacks * 2 * tail_cols, LANES)
    share = total_rows // n_y

    def chunk_of(k):
        start = ((y + k) % n_y) * share
        parts = [lax.dynamic_slice_in_dim(p, start, share, 0) for p in (gate_part, up_part)]
        return jnp.concatenate(parts, axis=1).astype(F32)

    own, tail = ring_sum(chunk_of, tail_part)
    hidden = gated(own[:, :main], own[:, hid : hid + main])
    hidden_main = lax.all_gather(hidden, "y", axis=0, tiled=True)
    tail = tail.reshape(stacks, 2 * tail_cols, LANES).transpose(1, 0, 2).reshape(2 * tail_cols, total_rows)
    hidden_tail = gated(tail[:tail_cols], tail[tail_cols:])

    produced = jnp.dot(hidden_main, w_down[0, :main], preferred_element_type=F32)
    produced = produced + lax.dot_general(
        hidden_tail, w_down[0, main:], (((0,), (0,)), ((), ())), preferred_element_type=F32
    )
    returned = exchange(produced.astype(BF).reshape(peers, slots, feat), CHIPS).reshape(total_rows, feat)

    partial = lax.dot_general(combine, returned, (((0,), (0,)), ((), ())), preferred_element_type=F32)
    partial = partial.reshape(n_c, tok, feat)
    mine = lax.dynamic_index_in_dim(partial, core, 0, keepdims=False)
    theirs = lax.dynamic_index_in_dim(partial, 1 - core, 0, keepdims=False).astype(BF)
    return (mine + lax.ppermute(theirs, "c", [(0, 1), (1, 0)]).astype(F32)).astype(BF)


def solution(mesh):
    n_group, n_inner, n_cuts = mesh.devices.shape
    fine = Mesh(mesh.devices.reshape(n_group, n_inner // 2, 2, n_cuts), ("x", "z", "c", "y"))
    owner = ("x", "z", "c")
    in_specs = (
        P(owner, "y"),
        P(owner, "y"),
        P(owner, None),
        P(owner, None),
        P(owner, "y", None),
        P(owner, "y", None),
        P(owner, None, "y"),
    )
    return jax.shard_map(per_device, mesh=fine, in_specs=in_specs, out_specs=P(owner, "y"), check_vma=False)
```

profile of v0, /device:TPU:1, one launch (start us, length us, event | category | flops | bytes accessed | tf_op | source)
XLA Modules:
  0.0 168.1 jit_solution(17167646480246003833)
XLA Ops:
  0.0 1.7 shard_map.73
  1.7 15.9 %all_gather.6 = bf16[64,640]{1,0:T(8,128)(2,1)S(1)} all-gather(bf16[32,640]{1,0:T(8,128)(2,1)} %shard_map.73), channel_id=1, replica_groups=mesh['x'=4,'z'=16,'c'=2,'y'=8] {'c'}, dimensions={0}, use_global_device_ids=true | all-gather | bytes 122880 | tf_op jit(solution)/shard_map/all_gather | solution.py:99
  18.3 1.2 fusion.1
  19.4 9.3 %all-to-all-start = ((bf16[64,8,512]{2,1,0:T(8,128)(2,1)}), bf16[64,8,512]{2,1,0:T(8,128)(2,1)S(1)}, u32[]{:S(2)}, u32[]{:S(2)}) async-start(bf16[64,8,512]{2,1,0:T(8,128)(2,1)} %fusion.1), calls=%async_computation | async-start | bytes 1048576 | tf_op jit(solution)/shard_map/all_to_all | solution.py:47
  29.3 29.2 %all-to-all-done = bf16[64,8,512]{2,1,0:T(8,128)(2,1)S(1)} async-done(((bf16[64,8,512]{2,1,0:T(8,128)(2,1)}), bf16[64,8,512]{2,1,0:T(8,128)(2,1)S(1)}, u32[]{:S(2)}, u32[]{:S(2)}) %all-to-all-start) | async-done | bytes 524320 | tf_op jit(solution)/shard_map/all_to_all | solution.py:47
  58.8 0.8 convolution_convert_fusion
  59.5 0.7 convolution_convert_fusion.1
  60.6 3.2 %collective-permute-start = (bf16[64,2176]{1,0:T(8,128)(2,1)S(1)}, bf16[64,2176]{1,0:T(8,128)(2,1)S(1)}, u32[]{:S(2)}, u32[]{:S(2)}) collective-permute-start(bf16[64,2176]{1,0:T(8,128)(2,1)S(1)} %get-tuple-element.23), channel_id=1, source_target_pairs={{0,1},{1,2},{2,3},{3,4},{4,5},{5,6},{6,7},{7,0},{8,9},{9,10},{10,1... | collective-permute-start | bytes 835592 | tf_op jit(solution)/shard_map/ppermute | solution.py:43
  63.9 3.8 %collective-permute-start.4 = (bf16[64,2176]{1,0:T(8,128)(2,1)S(1)}, bf16[64,2176]{1,0:T(8,128)(2,1)S(1)}, u32[]{:S(2)}, u32[]{:S(2)}) collective-permute-start(bf16[64,2176]{1,0:T(8,128)(2,1)S(1)} %get-tuple-element.24), channel_id=1, source_target_pairs={{0,7},{1,0},{2,1},{3,2},{4,3},{5,4},{6,5},{7,6},{8,15},{9,8},{10,9... | collective-permute-start | bytes 835592 | tf_op jit(solution)/shard_map/ppermute | solution.py:43
  67.7 2.0 %collective-permute-done = bf16[64,2176]{1,0:T(8,128)(2,1)S(1)} collective-permute-done((bf16[64,2176]{1,0:T(8,128)(2,1)S(1)}, bf16[64,2176]{1,0:T(8,128)(2,1)S(1)}, u32[]{:S(2)}, u32[]{:S(2)}) %collective-permute-start) | collective-permute-done | bytes 278560 | tf_op jit(solution)/shard_map/ppermute | solution.py:43
  69.8 1.9 %collective-permute-start.1 = (bf16[64,2176]{1,0:T(8,128)(2,1)S(1)}, bf16[64,2176]{1,0:T(8,128)(2,1)S(1)}, u32[]{:S(2)}, u32[]{:S(2)}) collective-permute-start(bf16[64,2176]{1,0:T(8,128)(2,1)S(1)} %pad_maximum_fusion.2), channel_id=1, source_target_pairs={{0,1},{1,2},{2,3},{3,4},{4,5},{5,6},{6,7},{7,0},{8,9},{9,10},{10,1... | collective-permute-start | bytes 835592 | tf_op jit(solution)/shard_map/ppermute | solution.py:43
  71.8 4.6 %collective-permute-start.5 = (bf16[64,2176]{1,0:T(8,128)(2,1)S(1)}, bf16[64,2176]{1,0:T(8,128)(2,1)S(1)}, u32[]{:S(2)}, u32[]{:S(2)}) collective-permute-start(bf16[64,2176]{1,0:T(8,128)(2,1)S(1)} %pad_maximum_fusion.5), channel_id=1, source_target_pairs={{0,7},{1,0},{2,1},{3,2},{4,3},{5,4},{6,5},{7,6},{8,15},{9,8},{10,9... | collective-permute-start | bytes 835592 | tf_op jit(solution)/shard_map/ppermute | solution.py:43
  76.4 1.9 %collective-permute-done.1 = bf16[64,2176]{1,0:T(8,128)(2,1)S(1)} collective-permute-done((bf16[64,2176]{1,0:T(8,128)(2,1)S(1)}, bf16[64,2176]{1,0:T(8,128)(2,1)S(1)}, u32[]{:S(2)}, u32[]{:S(2)}) %collective-permute-start.1) | collective-permute-done | bytes 278560 | tf_op jit(solution)/shard_map/ppermute | solution.py:43
  78.4 1.9 %collective-permute-start.2 = (bf16[64,2176]{1,0:T(8,128)(2,1)S(1)}, bf16[64,2176]{1,0:T(8,128)(2,1)S(1)}, u32[]{:S(2)}, u32[]{:S(2)}) collective-permute-start(bf16[64,2176]{1,0:T(8,128)(2,1)S(1)} %pad_maximum_fusion.3), channel_id=1, source_target_pairs={{0,1},{1,2},{2,3},{3,4},{4,5},{5,6},{6,7},{7,0},{8,9},{9,10},{10,1... | collective-permute-start | bytes 835592 | tf_op jit(solution)/shard_map/ppermute | solution.py:43
  80.4 4.6 %collective-permute-start.6 = (bf16[64,2176]{1,0:T(8,128)(2,1)S(1)}, bf16[64,2176]{1,0:T(8,128)(2,1)S(1)}, u32[]{:S(2)}, u32[]{:S(2)}) collective-permute-start(bf16[64,2176]{1,0:T(8,128)(2,1)S(1)} %pad_maximum_fusion.6), channel_id=1, source_target_pairs={{0,7},{1,0},{2,1},{3,2},{4,3},{5,4},{6,5},{7,6},{8,15},{9,8},{10,9... | collective-permute-start | bytes 835592 | tf_op jit(solution)/shard_map/ppermute | solution.py:43
  85.0 1.9 %collective-permute-done.2 = bf16[64,2176]{1,0:T(8,128)(2,1)S(1)} collective-permute-done((bf16[64,2176]{1,0:T(8,128)(2,1)S(1)}, bf16[64,2176]{1,0:T(8,128)(2,1)S(1)}, u32[]{:S(2)}, u32[]{:S(2)}) %collective-permute-start.2) | collective-permute-done | bytes 278560 | tf_op jit(solution)/shard_map/ppermute | solution.py:43
  87.0 1.9 %collective-permute-start.3 = (bf16[64,2176]{1,0:T(8,128)(2,1)S(1)}, bf16[64,2176]{1,0:T(8,128)(2,1)S(1)}, u32[]{:S(2)}, u32[]{:S(2)}) collective-permute-start(bf16[64,2176]{1,0:T(8,128)(2,1)S(1)} %pad_maximum_fusion.4), channel_id=1, source_target_pairs={{0,1},{1,2},{2,3},{3,4},{4,5},{5,6},{6,7},{7,0},{8,9},{9,10},{10,1... | collective-permute-start | bytes 835592 | tf_op jit(solution)/shard_map/ppermute | solution.py:43
  88.9 6.6 %collective-permute-done.3 = bf16[64,2176]{1,0:T(8,128)(2,1)S(1)} collective-permute-done((bf16[64,2176]{1,0:T(8,128)(2,1)S(1)}, bf16[64,2176]{1,0:T(8,128)(2,1)S(1)}, u32[]{:S(2)}, u32[]{:S(2)}) %collective-permute-start.3) | collective-permute-done | bytes 278560 | tf_op jit(solution)/shard_map/ppermute | solution.py:43
  95.7 22.9 %all_gather.7 = bf16[512,1016]{1,0:T(8,128)(2,1)S(1)} all-gather(bf16[64,1016]{1,0:T(8,128)(2,1)S(1)} %fusion.15), channel_id=1, replica_groups=mesh['x'=4,'z'=16,'c'=2,'y'=8] {'y'}, dimensions={0}, use_global_device_ids=true | all-gather | bytes 1170432 | tf_op jit(solution)/shard_map/all_gather | solution.py:134
  119.3 1.2 fusion.2
  120.5 11.1 %all-to-all-start.1 = ((bf16[64,8,512]{2,1,0:T(8,128)(2,1)}), bf16[64,8,512]{2,1,0:T(8,128)(2,1)S(1)}, u32[]{:S(2)}, u32[]{:S(2)}) async-start(bf16[64,8,512]{2,1,0:T(8,128)(2,1)} %fusion.2), calls=%async_computation.1 | async-start | bytes 1048576 | tf_op jit(solution)/shard_map/all_to_all | solution.py:47
  132.2 19.7 %all-to-all-done.1 = bf16[64,8,512]{2,1,0:T(8,128)(2,1)S(1)} async-done(((bf16[64,8,512]{2,1,0:T(8,128)(2,1)}), bf16[64,8,512]{2,1,0:T(8,128)(2,1)S(1)}, u32[]{:S(2)}, u32[]{:S(2)}) %all-to-all-start.1) | async-done | bytes 524320 | tf_op jit(solution)/shard_map/all_to_all | solution.py:47
  152.1 14.5 %collective-permute-start.7 = (bf16[32,512]{1,0:T(8,128)(2,1)S(1)}, bf16[32,512]{1,0:T(8,128)(2,1)S(1)}, u32[]{:S(2)}, u32[]{:S(2)}) collective-permute-start(bf16[32,512]{1,0:T(8,128)(2,1)S(1)} %fusion.22), channel_id=1, source_target_pairs={{0,8},{8,0},{1,9},{9,1},{2,10},{10,2},{3,11},{11,3},{4,12},{12,4},... | collective-permute-start | bytes 98312 | tf_op jit(solution)/shard_map/ppermute | solution.py:148
  166.6 0.8 collective-permute-done.7
  (55 shorter events, 4.5 us)
Async XLA Ops:
  18.1 10.8 %copy-start = (bf16[1,512,1024]{2,1,0:T(8,128)(2,1)S(1)}, bf16[1,512,1024]{2,1,0:T(8,128)(2,1)}, u32[]{:S(2)}) copy-start(bf16[1,512,1024]{2,1,0:T(8,128)(2,1)} %param.12) | copy-start | bytes 3145732
  18.3 10.8 %copy-start.1 = (bf16[1,512,1024]{2,1,0:T(8,128)(2,1)S(1)}, bf16[1,512,1024]{2,1,0:T(8,128)(2,1)}, u32[]{:S(2)}) copy-start(bf16[1,512,1024]{2,1,0:T(8,128)(2,1)} %param.11) | copy-start | bytes 3145732
  19.4 39.1 %all-to-all-start = ((bf16[64,8,512]{2,1,0:T(8,128)(2,1)}), bf16[64,8,512]{2,1,0:T(8,128)(2,1)S(1)}, u32[]{:S(2)}, u32[]{:S(2)}) async-start(bf16[64,8,512]{2,1,0:T(8,128)(2,1)} %fusion.1), calls=%async_computation | async-start | bytes 1048576 | tf_op jit(solution)/shard_map/all_to_all | solution.py:47
  60.6 9.0 %collective-permute-start = (bf16[64,2176]{1,0:T(8,128)(2,1)S(1)}, bf16[64,2176]{1,0:T(8,128)(2,1)S(1)}, u32[]{:S(2)}, u32[]{:S(2)}) collective-permute-start(bf16[64,2176]{1,0:T(8,128)(2,1)S(1)} %get-tuple-element.23), channel_id=1, source_target_pairs={{0,1},{1,2},{2,3},{3,4},{4,5},{5,6},{6,7},{7,0},{8,9},{9,10},{10,1... | collective-permute-start | bytes 835592 | tf_op jit(solution)/shard_map/ppermute | solution.py:43
  63.9 7.8 %collective-permute-start.4 = (bf16[64,2176]{1,0:T(8,128)(2,1)S(1)}, bf16[64,2176]{1,0:T(8,128)(2,1)S(1)}, u32[]{:S(2)}, u32[]{:S(2)}) collective-permute-start(bf16[64,2176]{1,0:T(8,128)(2,1)S(1)} %get-tuple-element.24), channel_id=1, source_target_pairs={{0,7},{1,0},{2,1},{3,2},{4,3},{5,4},{6,5},{7,6},{8,15},{9,8},{10,9... | collective-permute-start | bytes 835592 | tf_op jit(solution)/shard_map/ppermute | solution.py:43
  69.8 8.5 %collective-permute-start.1 = (bf16[64,2176]{1,0:T(8,128)(2,1)S(1)}, bf16[64,2176]{1,0:T(8,128)(2,1)S(1)}, u32[]{:S(2)}, u32[]{:S(2)}) collective-permute-start(bf16[64,2176]{1,0:T(8,128)(2,1)S(1)} %pad_maximum_fusion.2), channel_id=1, source_target_pairs={{0,1},{1,2},{2,3},{3,4},{4,5},{5,6},{6,7},{7,0},{8,9},{9,10},{10,1... | collective-permute-start | bytes 835592 | tf_op jit(solution)/shard_map/ppermute | solution.py:43
  71.8 8.5 %collective-permute-start.5 = (bf16[64,2176]{1,0:T(8,128)(2,1)S(1)}, bf16[64,2176]{1,0:T(8,128)(2,1)S(1)}, u32[]{:S(2)}, u32[]{:S(2)}) collective-permute-start(bf16[64,2176]{1,0:T(8,128)(2,1)S(1)} %pad_maximum_fusion.5), channel_id=1, source_target_pairs={{0,7},{1,0},{2,1},{3,2},{4,3},{5,4},{6,5},{7,6},{8,15},{9,8},{10,9... | collective-permute-start | bytes 835592 | tf_op jit(solution)/shard_map/ppermute | solution.py:43
  78.4 8.5 %collective-permute-start.2 = (bf16[64,2176]{1,0:T(8,128)(2,1)S(1)}, bf16[64,2176]{1,0:T(8,128)(2,1)S(1)}, u32[]{:S(2)}, u32[]{:S(2)}) collective-permute-start(bf16[64,2176]{1,0:T(8,128)(2,1)S(1)} %pad_maximum_fusion.3), channel_id=1, source_target_pairs={{0,1},{1,2},{2,3},{3,4},{4,5},{5,6},{6,7},{7,0},{8,9},{9,10},{10,1... | collective-permute-start | bytes 835592 | tf_op jit(solution)/shard_map/ppermute | solution.py:43
  80.4 8.5 %collective-permute-start.6 = (bf16[64,2176]{1,0:T(8,128)(2,1)S(1)}, bf16[64,2176]{1,0:T(8,128)(2,1)S(1)}, u32[]{:S(2)}, u32[]{:S(2)}) collective-permute-start(bf16[64,2176]{1,0:T(8,128)(2,1)S(1)} %pad_maximum_fusion.6), channel_id=1, source_target_pairs={{0,7},{1,0},{2,1},{3,2},{4,3},{5,4},{6,5},{7,6},{8,15},{9,8},{10,9... | collective-permute-start | bytes 835592 | tf_op jit(solution)/shard_map/ppermute | solution.py:43
  87.0 8.5 %collective-permute-start.3 = (bf16[64,2176]{1,0:T(8,128)(2,1)S(1)}, bf16[64,2176]{1,0:T(8,128)(2,1)S(1)}, u32[]{:S(2)}, u32[]{:S(2)}) collective-permute-start(bf16[64,2176]{1,0:T(8,128)(2,1)S(1)} %pad_maximum_fusion.4), channel_id=1, source_target_pairs={{0,1},{1,2},{2,3},{3,4},{4,5},{5,6},{6,7},{7,0},{8,9},{9,10},{10,1... | collective-permute-start | bytes 835592 | tf_op jit(solution)/shard_map/ppermute | solution.py:43
  95.6 23.0 %copy-start.2 = (bf16[1,1024,512]{2,1,0:T(8,128)(2,1)S(1)}, bf16[1,1024,512]{2,1,0:T(8,128)(2,1)}, u32[]{:S(2)}) copy-start(bf16[1,1024,512]{2,1,0:T(8,128)(2,1)} %param.13) | copy-start | bytes 3145732
  120.5 31.4 %all-to-all-start.1 = ((bf16[64,8,512]{2,1,0:T(8,128)(2,1)}), bf16[64,8,512]{2,1,0:T(8,128)(2,1)S(1)}, u32[]{:S(2)}, u32[]{:S(2)}) async-start(bf16[64,8,512]{2,1,0:T(8,128)(2,1)} %fusion.2), calls=%async_computation.1 | async-start | bytes 1048576 | tf_op jit(solution)/shard_map/all_to_all | solution.py:47
  152.1 15.3 %collective-permute-start.7 = (bf16[32,512]{1,0:T(8,128)(2,1)S(1)}, bf16[32,512]{1,0:T(8,128)(2,1)S(1)}, u32[]{:S(2)}, u32[]{:S(2)}) collective-permute-start(bf16[32,512]{1,0:T(8,128)(2,1)S(1)} %fusion.22), channel_id=1, source_target_pairs={{0,8},{8,0},{1,9},{9,1},{2,10},{10,2},{3,11},{11,3},{4,12},{12,4},... | collective-permute-start | bytes 98312 | tf_op jit(solution)/shard_map/ppermute | solution.py:148
where the time goes:
time: 169 us; the launch traced here: 168 us
  waiting for transfers between devices  62.1 us (37%)
  starting transfers between devices  56.8 us (34%)
  blocking collectives  38.7 us (23%)
  matrix products  4.94 us (3%)
  other arithmetic  2.08 us (1%)
    all_to_all x2, waiting for transfers between devices, exchange(): return lax.all_to_all(value, axis, split_axis=0, concat_axis=0, tiled=True)  49 us
    all_gather x1, blocking collectives, per_device(): hidden_main = lax.all_gather(hidden, 'y', axis=0, tiled=True)  22.9 us
    ppermute x7, starting transfers between devices, along(): lax.ppermute(value, 'y', [(i, (i + step) % size) for i in range(size)])  21.9 us
    all_to_all x2, starting transfers between devices, exchange(): return lax.all_to_all(value, axis, split_axis=0, concat_axis=0, tiled=True)  20.4 us
    all_gather x1, blocking collectives, per_device(): pair = lax.all_gather(message, 'c', axis=0, tiled=True)  15.9 us
    ppermute x1, starting transfers between devices, per_device(): lax.ppermute(theirs, 'c', [(0, 1), (1, 0)]).astype(F32)  14.5 us
    ppermute x7, waiting for transfers between devices, along(): lax.ppermute(value, 'y', [(i, (i + step) % size) for i in range(size)])  12.3 us
  transfers between devices with their start and end apart: 10, of which 7 were waited for; matrix products, arithmetic and copies ran while one was open for 1% of the time, Pallas kernels for 0%

commit v1 on v0

--- a/solution.py
+++ b/solution.py
@@ -2,7 +2,6 @@
 import jax.numpy as jnp
 from jax import lax
 from jax.experimental import pallas as pl
-from jax.experimental.pallas import tpu as pltpu
 from jax.sharding import Mesh, PartitionSpec as P
 
 CAP = 4
@@ -135,17 +134,17 @@
     tail = tail.reshape(stacks, 2 * tail_cols, LANES).transpose(1, 0, 2).reshape(2 * tail_cols, total_rows)
     hidden_tail = gated(tail[:tail_cols], tail[tail_cols:])
 
-    produced = jnp.dot(hidden_main, w_down[0, :main], preferred_element_type=F32)
-    produced = produced + lax.dot_general(
-        hidden_tail, w_down[0, main:], (((0,), (0,)), ((), ())), preferred_element_type=F32
-    )
+    hidden_all = jnp.concatenate([hidden_main, hidden_tail.T], axis=1)
+    produced = jnp.dot(hidden_all, w_down[0], preferred_element_type=F32)
     returned = exchange(produced.astype(BF).reshape(peers, slots, feat), CHIPS).reshape(total_rows, feat)
 
     partial = lax.dot_general(combine, returned, (((0,), (0,)), ((), ())), preferred_element_type=F32)
     partial = partial.reshape(n_c, tok, feat)
     mine = lax.dynamic_index_in_dim(partial, core, 0, keepdims=False)
     theirs = lax.dynamic_index_in_dim(partial, 1 - core, 0, keepdims=False).astype(BF)
-    return (mine + lax.ppermute(theirs, "c", [(0, 1), (1, 0)]).astype(F32)).astype(BF)
+    crossed = lax.all_gather(theirs, "c", axis=0, tiled=False)
+    crossed = lax.dynamic_index_in_dim(crossed, 1 - core, 0, keepdims=False)
+    return (mine + crossed.astype(F32)).astype(BF)
 
 
 def solution(mesh):

time: 169 us -> 168 us (level)
  starting transfers between devices: 56.8 us -> 42.4 us
  blocking collectives: 38.7 us -> 52.6 us
  waiting for transfers between devices: 62.1 us -> 60.4 us
    ppermute x1 -> x0, starting transfers between devices: 14.5 us -> none  [per_device(): lax.ppermute(theirs, 'c', [(0, 1), (1, 0)]).astype(F32)]
    all_gather x0 -> x1, blocking collectives: none -> 14.1 us  [per_device(): crossed = lax.all_gather(theirs, 'c', axis=0, tiled=False)]
  transfers between devices with their start and end apart: 10 -> 9, of which waited for: 7 -> 6; matrix products, arithmetic and copies ran while one was open for 1% -> 1% of each run, Pallas kernels for 0% -> 0%
where the time goes in v1:
time: 168 us; the launch traced here: 167 us
  waiting for transfers between devices  60.4 us (36%)
  blocking collectives  52.6 us (31%)
  starting transfers between devices  42.4 us (25%)
  matrix products  4.55 us (3%)
  local copies, waits for them, and re-layouts  2.84 us (2%)
  other arithmetic  2.1 us (1%)
  Pallas kernels  1.75 us (1%)
    all_to_all x2, waiting for transfers between devices, exchange(): return lax.all_to_all(value, axis, split_axis=0, concat_axis=0, tiled=True)  48.1 us
    all_gather x1, blocking collectives, per_device(): hidden_main = lax.all_gather(hidden, 'y', axis=0, tiled=True)  22.7 us
    ppermute x7, starting transfers between devices, along(): lax.ppermute(value, 'y', [(i, (i + step) % size) for i in range(size)])  21.9 us
    all_to_all x2, starting transfers between devices, exchange(): return lax.all_to_all(value, axis, split_axis=0, concat_axis=0, tiled=True)  20.5 us
    all_gather x1, blocking collectives, per_device(): pair = lax.all_gather(message, 'c', axis=0, tiled=True)  15.9 us
    all_gather x1, blocking collectives, per_device(): crossed = lax.all_gather(theirs, 'c', axis=0, tiled=False)  14.1 us
    ppermute x7, waiting for transfers between devices, along(): lax.ppermute(value, 'y', [(i, (i + step) % size) for i in range(size)])  12.3 us
  transfers between devices with their start and end apart: 9, of which 6 were waited for; matrix products, arithmetic and copies ran while one was open for 1% of the time, Pallas kernels for 0%

profile of v1, /device:TPU:1, one launch (start us, length us, event | category | flops | bytes accessed | tf_op | source)
XLA Modules:
  0.0 167.1 jit_solution(14318581432296174660)
XLA Ops:
  0.0 1.8 %shard_map.73 = bf16[32,640]{1,0:T(8,128)(2,1)} custom-call(bf16[32,512]{1,0:T(8,128)(2,1)} %tokens_ref.1, s32[4,32]{1,0:T(4,128)} %bitcast.97, s32[8,32]{1,0:T(8,128)} %bitcast.95, f32[8,32]{1,0:T(8,128)} %bitcast.96), custom_call_target="tpu_custom_call" | custom-call | tf_op jit(solution)/shard_map/pallas_call | solution.py:34
  1.8 15.9 %all_gather.10 = bf16[64,640]{1,0:T(8,128)(2,1)S(1)} all-gather(bf16[32,640]{1,0:T(8,128)(2,1)} %shard_map.73), channel_id=1, replica_groups=mesh['x'=4,'z'=16,'c'=2,'y'=8] {'c'}, dimensions={0}, use_global_device_ids=true | all-gather | bytes 122880 | tf_op jit(solution)/shard_map/all_gather | solution.py:98
  18.4 1.2 fusion.1
  19.5 9.3 %all-to-all-start = ((bf16[64,8,512]{2,1,0:T(8,128)(2,1)}), bf16[64,8,512]{2,1,0:T(8,128)(2,1)S(1)}, u32[]{:S(2)}, u32[]{:S(2)}) async-start(bf16[64,8,512]{2,1,0:T(8,128)(2,1)} %fusion.1), calls=%async_computation | async-start | bytes 1048576 | tf_op jit(solution)/shard_map/all_to_all | solution.py:46
  29.2 1.0 slice.83
  30.3 28.3 %all-to-all-done = bf16[64,8,512]{2,1,0:T(8,128)(2,1)S(1)} async-done(((bf16[64,8,512]{2,1,0:T(8,128)(2,1)}), bf16[64,8,512]{2,1,0:T(8,128)(2,1)S(1)}, u32[]{:S(2)}, u32[]{:S(2)}) %all-to-all-start) | async-done | bytes 524320 | tf_op jit(solution)/shard_map/all_to_all | solution.py:46
  58.9 0.7 convolution_convert_fusion
  60.1 0.7 convolution_convert_fusion.1
  61.2 3.2 %collective-permute-start = (bf16[64,2176]{1,0:T(8,128)(2,1)S(1)}, bf16[64,2176]{1,0:T(8,128)(2,1)S(1)}, u32[]{:S(2)}, u32[]{:S(2)}) collective-permute-start(bf16[64,2176]{1,0:T(8,128)(2,1)S(1)} %get-tuple-element.24), channel_id=1, source_target_pairs={{0,1},{1,2},{2,3},{3,4},{4,5},{5,6},{6,7},{7,0},{8,9},{9,10},{10,1... | collective-permute-start | bytes 835592 | tf_op jit(solution)/shard_map/ppermute | solution.py:42
  64.4 3.8 %collective-permute-start.4 = (bf16[64,2176]{1,0:T(8,128)(2,1)S(1)}, bf16[64,2176]{1,0:T(8,128)(2,1)S(1)}, u32[]{:S(2)}, u32[]{:S(2)}) collective-permute-start(bf16[64,2176]{1,0:T(8,128)(2,1)S(1)} %get-tuple-element.23), channel_id=1, source_target_pairs={{0,7},{1,0},{2,1},{3,2},{4,3},{5,4},{6,5},{7,6},{8,15},{9,8},{10,9... | collective-permute-start | bytes 835592 | tf_op jit(solution)/shard_map/ppermute | solution.py:42
  68.2 2.0 %collective-permute-done = bf16[64,2176]{1,0:T(8,128)(2,1)S(1)} collective-permute-done((bf16[64,2176]{1,0:T(8,128)(2,1)S(1)}, bf16[64,2176]{1,0:T(8,128)(2,1)S(1)}, u32[]{:S(2)}, u32[]{:S(2)}) %collective-permute-start) | collective-permute-done | bytes 278560 | tf_op jit(solution)/shard_map/ppermute | solution.py:42
  70.3 1.9 %collective-permute-start.1 = (bf16[64,2176]{1,0:T(8,128)(2,1)S(1)}, bf16[64,2176]{1,0:T(8,128)(2,1)S(1)}, u32[]{:S(2)}, u32[]{:S(2)}) collective-permute-start(bf16[64,2176]{1,0:T(8,128)(2,1)S(1)} %pad_maximum_fusion.2), channel_id=1, source_target_pairs={{0,1},{1,2},{2,3},{3,4},{4,5},{5,6},{6,7},{7,0},{8,9},{9,10},{10,1... | collective-permute-start | bytes 835592 | tf_op jit(solution)/shard_map/ppermute | solution.py:42
  72.4 4.6 %collective-permute-start.5 = (bf16[64,2176]{1,0:T(8,128)(2,1)S(1)}, bf16[64,2176]{1,0:T(8,128)(2,1)S(1)}, u32[]{:S(2)}, u32[]{:S(2)}) collective-permute-start(bf16[64,2176]{1,0:T(8,128)(2,1)S(1)} %pad_maximum_fusion.5), channel_id=1, source_target_pairs={{0,7},{1,0},{2,1},{3,2},{4,3},{5,4},{6,5},{7,6},{8,15},{9,8},{10,9... | collective-permute-start | bytes 835592 | tf_op jit(solution)/shard_map/ppermute | solution.py:42
  77.0 1.9 %collective-permute-done.1 = bf16[64,2176]{1,0:T(8,128)(2,1)S(1)} collective-permute-done((bf16[64,2176]{1,0:T(8,128)(2,1)S(1)}, bf16[64,2176]{1,0:T(8,128)(2,1)S(1)}, u32[]{:S(2)}, u32[]{:S(2)}) %collective-permute-start.1) | collective-permute-done | bytes 278560 | tf_op jit(solution)/shard_map/ppermute | solution.py:42
  78.9 1.9 %collective-permute-start.2 = (bf16[64,2176]{1,0:T(8,128)(2,1)S(1)}, bf16[64,2176]{1,0:T(8,128)(2,1)S(1)}, u32[]{:S(2)}, u32[]{:S(2)}) collective-permute-start(bf16[64,2176]{1,0:T(8,128)(2,1)S(1)} %pad_maximum_fusion.3), channel_id=1, source_target_pairs={{0,1},{1,2},{2,3},{3,4},{4,5},{5,6},{6,7},{7,0},{8,9},{9,10},{10,1... | collective-permute-start | bytes 835592 | tf_op jit(solution)/shard_map/ppermute | solution.py:42
  81.0 4.6 %collective-permute-start.6 = (bf16[64,2176]{1,0:T(8,128)(2,1)S(1)}, bf16[64,2176]{1,0:T(8,128)(2,1)S(1)}, u32[]{:S(2)}, u32[]{:S(2)}) collective-permute-start(bf16[64,2176]{1,0:T(8,128)(2,1)S(1)} %pad_maximum_fusion.6), channel_id=1, source_target_pairs={{0,7},{1,0},{2,1},{3,2},{4,3},{5,4},{6,5},{7,6},{8,15},{9,8},{10,9... | collective-permute-start | bytes 835592 | tf_op jit(solution)/shard_map/ppermute | solution.py:42
  85.6 1.9 %collective-permute-done.2 = bf16[64,2176]{1,0:T(8,128)(2,1)S(1)} collective-permute-done((bf16[64,2176]{1,0:T(8,128)(2,1)S(1)}, bf16[64,2176]{1,0:T(8,128)(2,1)S(1)}, u32[]{:S(2)}, u32[]{:S(2)}) %collective-permute-start.2) | collective-permute-done | bytes 278560 | tf_op jit(solution)/shard_map/ppermute | solution.py:42
  87.5 1.9 %collective-permute-start.3 = (bf16[64,2176]{1,0:T(8,128)(2,1)S(1)}, bf16[64,2176]{1,0:T(8,128)(2,1)S(1)}, u32[]{:S(2)}, u32[]{:S(2)}) collective-permute-start(bf16[64,2176]{1,0:T(8,128)(2,1)S(1)} %pad_maximum_fusion.4), channel_id=1, source_target_pairs={{0,1},{1,2},{2,3},{3,4},{4,5},{5,6},{6,7},{7,0},{8,9},{9,10},{10,1... | collective-permute-start | bytes 835592 | tf_op jit(solution)/shard_map/ppermute | solution.py:42
  89.5 6.6 %collective-permute-done.3 = bf16[64,2176]{1,0:T(8,128)(2,1)S(1)} collective-permute-done((bf16[64,2176]{1,0:T(8,128)(2,1)S(1)}, bf16[64,2176]{1,0:T(8,128)(2,1)S(1)}, u32[]{:S(2)}, u32[]{:S(2)}) %collective-permute-start.3) | collective-permute-done | bytes 278560 | tf_op jit(solution)/shard_map/ppermute | solution.py:42
  96.4 22.7 %all_gather.11 = bf16[512,1016]{1,0:T(8,128)(2,1)S(1)} all-gather(bf16[64,1016]{1,0:T(8,128)(2,1)S(1)} %fusion.15), channel_id=1, replica_groups=mesh['x'=4,'z'=16,'c'=2,'y'=8] {'y'}, dimensions={0}, use_global_device_ids=true | all-gather | bytes 1170432 | tf_op jit(solution)/shard_map/all_gather | solution.py:133
  119.1 1.5 fusion
  120.7 11.2 %all-to-all-start.1 = ((bf16[64,8,512]{2,1,0:T(8,128)(2,1)}), bf16[64,8,512]{2,1,0:T(8,128)(2,1)S(1)}, u32[]{:S(2)}, u32[]{:S(2)}) async-start(bf16[64,8,512]{2,1,0:T(8,128)(2,1)} %fusion), calls=%async_computation.1 | async-start | bytes 1048576 | tf_op jit(solution)/shard_map/all_to_all | solution.py:46
  132.4 19.7 %all-to-all-done.1 = bf16[64,8,512]{2,1,0:T(8,128)(2,1)S(1)} async-done(((bf16[64,8,512]{2,1,0:T(8,128)(2,1)}), bf16[64,8,512]{2,1,0:T(8,128)(2,1)S(1)}, u32[]{:S(2)}, u32[]{:S(2)}) %all-to-all-start.1) | async-done | bytes 524320 | tf_op jit(solution)/shard_map/all_to_all | solution.py:46
  152.4 14.1 %all_gather.12 = bf16[2,32,512]{2,1,0:T(8,128)(2,1)S(1)} all-gather(bf16[1,32,512]{2,1,0:T(8,128)(2,1)S(1)} %dynamic-slice_convert_fusion), channel_id=1, replica_groups=mesh['x'=4,'z'=16,'c'=2,'y'=8] {'c'}, dimensions={0}, use_global_device_ids=true | all-gather | bytes 98304 | tf_op jit(solution)/shard_map/all_gather | solution.py:145
  (55 shorter events, 4.4 us)
Async XLA Ops:
  0.0 119.1 %copy-start = (bf16[1,1024,512]{2,1,0:T(8,128)(2,1)S(1)}, bf16[1,1024,512]{2,1,0:T(8,128)(2,1)}, u32[]{:S(2)}) copy-start(bf16[1,1024,512]{2,1,0:T(8,128)(2,1)} %param.13) | copy-start | bytes 3145732
  18.2 10.8 %copy-start.1 = (bf16[1,512,1024]{2,1,0:T(8,128)(2,1)S(1)}, bf16[1,512,1024]{2,1,0:T(8,128)(2,1)}, u32[]{:S(2)}) copy-start(bf16[1,512,1024]{2,1,0:T(8,128)(2,1)} %param.12) | copy-start | bytes 3145732
  19.5 39.1 %all-to-all-start = ((bf16[64,8,512]{2,1,0:T(8,128)(2,1)}), bf16[64,8,512]{2,1,0:T(8,128)(2,1)S(1)}, u32[]{:S(2)}, u32[]{:S(2)}) async-start(bf16[64,8,512]{2,1,0:T(8,128)(2,1)} %fusion.1), calls=%async_computation | async-start | bytes 1048576 | tf_op jit(solution)/shard_map/all_to_all | solution.py:46
  58.8 1.2 copy-start.2
  61.2 9.0 %collective-permute-start = (bf16[64,2176]{1,0:T(8,128)(2,1)S(1)}, bf16[64,2176]{1,0:T(8,128)(2,1)S(1)}, u32[]{:S(2)}, u32[]{:S(2)}) collective-permute-start(bf16[64,2176]{1,0:T(8,128)(2,1)S(1)} %get-tuple-element.24), channel_id=1, source_target_pairs={{0,1},{1,2},{2,3},{3,4},{4,5},{5,6},{6,7},{7,0},{8,9},{9,10},{10,1... | collective-permute-start | bytes 835592 | tf_op jit(solution)/shard_map/ppermute | solution.py:42
  64.4 7.8 %collective-permute-start.4 = (bf16[64,2176]{1,0:T(8,128)(2,1)S(1)}, bf16[64,2176]{1,0:T(8,128)(2,1)S(1)}, u32[]{:S(2)}, u32[]{:S(2)}) collective-permute-start(bf16[64,2176]{1,0:T(8,128)(2,1)S(1)} %get-tuple-element.23), channel_id=1, source_target_pairs={{0,7},{1,0},{2,1},{3,2},{4,3},{5,4},{6,5},{7,6},{8,15},{9,8},{10,9... | collective-permute-start | bytes 835592 | tf_op jit(solution)/shard_map/ppermute | solution.py:42
  70.3 8.5 %collective-permute-start.1 = (bf16[64,2176]{1,0:T(8,128)(2,1)S(1)}, bf16[64,2176]{1,0:T(8,128)(2,1)S(1)}, u32[]{:S(2)}, u32[]{:S(2)}) collective-permute-start(bf16[64,2176]{1,0:T(8,128)(2,1)S(1)} %pad_maximum_fusion.2), channel_id=1, source_target_pairs={{0,1},{1,2},{2,3},{3,4},{4,5},{5,6},{6,7},{7,0},{8,9},{9,10},{10,1... | collective-permute-start | bytes 835592 | tf_op jit(solution)/shard_map/ppermute | solution.py:42
  72.4 8.5 %collective-permute-start.5 = (bf16[64,2176]{1,0:T(8,128)(2,1)S(1)}, bf16[64,2176]{1,0:T(8,128)(2,1)S(1)}, u32[]{:S(2)}, u32[]{:S(2)}) collective-permute-start(bf16[64,2176]{1,0:T(8,128)(2,1)S(1)} %pad_maximum_fusion.5), channel_id=1, source_target_pairs={{0,7},{1,0},{2,1},{3,2},{4,3},{5,4},{6,5},{7,6},{8,15},{9,8},{10,9... | collective-permute-start | bytes 835592 | tf_op jit(solution)/shard_map/ppermute | solution.py:42
  78.9 8.5 %collective-permute-start.2 = (bf16[64,2176]{1,0:T(8,128)(2,1)S(1)}, bf16[64,2176]{1,0:T(8,128)(2,1)S(1)}, u32[]{:S(2)}, u32[]{:S(2)}) collective-permute-start(bf16[64,2176]{1,0:T(8,128)(2,1)S(1)} %pad_maximum_fusion.3), channel_id=1, source_target_pairs={{0,1},{1,2},{2,3},{3,4},{4,5},{5,6},{6,7},{7,0},{8,9},{9,10},{10,1... | collective-permute-start | bytes 835592 | tf_op jit(solution)/shard_map/ppermute | solution.py:42
  81.0 8.5 %collective-permute-start.6 = (bf16[64,2176]{1,0:T(8,128)(2,1)S(1)}, bf16[64,2176]{1,0:T(8,128)(2,1)S(1)}, u32[]{:S(2)}, u32[]{:S(2)}) collective-permute-start(bf16[64,2176]{1,0:T(8,128)(2,1)S(1)} %pad_maximum_fusion.6), channel_id=1, source_target_pairs={{0,7},{1,0},{2,1},{3,2},{4,3},{5,4},{6,5},{7,6},{8,15},{9,8},{10,9... | collective-permute-start | bytes 835592 | tf_op jit(solution)/shard_map/ppermute | solution.py:42
  87.5 8.5 %collective-permute-start.3 = (bf16[64,2176]{1,0:T(8,128)(2,1)S(1)}, bf16[64,2176]{1,0:T(8,128)(2,1)S(1)}, u32[]{:S(2)}, u32[]{:S(2)}) collective-permute-start(bf16[64,2176]{1,0:T(8,128)(2,1)S(1)} %pad_maximum_fusion.4), channel_id=1, source_target_pairs={{0,1},{1,2},{2,3},{3,4},{4,5},{5,6},{6,7},{7,0},{8,9},{9,10},{10,1... | collective-permute-start | bytes 835592 | tf_op jit(solution)/shard_map/ppermute | solution.py:42
  120.7 31.5 %all-to-all-start.1 = ((bf16[64,8,512]{2,1,0:T(8,128)(2,1)}), bf16[64,8,512]{2,1,0:T(8,128)(2,1)S(1)}, u32[]{:S(2)}, u32[]{:S(2)}) async-start(bf16[64,8,512]{2,1,0:T(8,128)(2,1)} %fusion), calls=%async_computation.1 | async-start | bytes 1048576 | tf_op jit(solution)/shard_map/all_to_all | solution.py:46

commit v2 on v1

--- a/solution.py
+++ b/solution.py
@@ -48,35 +48,38 @@
 
 def ring_sum(chunk_of, extra):
     size = lax.axis_size("y")
-    right, left = size // 2, (size - 1) // 2
+    steps = size // 2
     width = chunk_of(0).shape[1]
+    half = width // 2
 
-    def join(k, arrived, block):
-        part = chunk_of(k)
-        if arrived is not None:
-            part = part + arrived[:, :width].astype(F32)
+    def join(part, block):
         return jnp.concatenate([part.astype(BF), block], axis=1)
 
     total = extra.astype(F32)
-    to_right = join(right, None, extra) if right else None
-    to_left = join(-left, None, extra) if left else None
-    for step in range(right):
+    farthest = chunk_of(steps)
+    to_right = join(farthest[:, :half], extra)
+    to_left = join(farthest[:, half:], extra)
+    for step in range(steps):
         to_right = along(to_right, 1)
-        if step < left:
-            to_left = along(to_left, -1)
-        total = total + to_right[:, width:].astype(F32)
-        if step < left:
-            total = total + to_left[:, width:].astype(F32)
-        if step < right - 1:
-            to_right = join(right - 1 - step, to_right, to_right[:, width:])
-        if step < left - 1:
-            to_left = join(step + 1 - left, to_left, to_left[:, width:])
-    own = chunk_of(0)
-    if right:
-        own = own + to_right[:, :width].astype(F32)
-    if left:
-        own = own + to_left[:, :width].astype(F32)
-    return own, total
+        to_left = along(to_left, -1)
+        right_block = to_right[:, -extra.shape[1] :]
+        total = total + right_block.astype(F32)
+        last = step == steps - 1
+        if not last:
+            left_block = to_left[:, -extra.shape[1] :]
+            total = total + left_block.astype(F32)
+        k = steps - 1 - step
+        ahead, behind = chunk_of(k), chunk_of(-k)
+        if step == 0:
+            ahead = jnp.concatenate([ahead[:, :half] + to_right[:, :half].astype(F32), ahead[:, half:]], axis=1)
+            behind = jnp.concatenate([behind[:, :half], behind[:, half:] + to_left[:, :half].astype(F32)], axis=1)
+        elif not last:
+            ahead = ahead + to_right[:, :width].astype(F32)
+            behind = behind + to_left[:, :width].astype(F32)
+        if not last:
+            to_right = join(ahead, right_block)
+            to_left = join(behind, left_block) if step < steps - 2 else behind.astype(BF)
+    return chunk_of(0) + to_right[:, :width].astype(F32) + to_left[:, :width].astype(F32), total
 
 
 def gated(gate, up):

time: 168 us -> 167 us (level)
  waiting for transfers between devices: 60.4 us -> 55.7 us
  starting transfers between devices: 42.4 us -> 45.8 us
    ppermute x7 -> x8, waiting for transfers between devices: 12.3 us -> 7.67 us  [along(): lax.ppermute(value, 'y', [(i, (i + step) % size) for i in range(size)])]
    ppermute x7 -> x8, starting transfers between devices: 21.9 us -> 26.5 us  [along(): lax.ppermute(value, 'y', [(i, (i + step) % size) for i in range(size)])]
  transfers between devices with their start and end apart: 9 -> 10, of which waited for: 6 -> 7; matrix products, arithmetic and copies ran while one was open for 1% -> 2% of each run, Pallas kernels for 0% -> 0%
where the time goes in v2:
time: 167 us; the launch traced here: 166 us
  waiting for transfers between devices  55.7 us (33%)
  blocking collectives  52.9 us (32%)
  starting transfers between devices  45.8 us (27%)
  matrix products  4.54 us (3%)
  local copies, waits for them, and re-layouts  2.71 us (2%)
  other arithmetic  2.09 us (1%)
  Pallas kernels  1.76 us (1%)
    all_to_all x2, waiting for transfers between devices, exchange(): return lax.all_to_all(value, axis, split_axis=0, concat_axis=0, tiled=True)  48.1 us
    ppermute x8, starting transfers between devices, along(): lax.ppermute(value, 'y', [(i, (i + step) % size) for i in range(size)])  26.5 us
    all_gather x1, blocking collectives, per_device(): hidden_main = lax.all_gather(hidden, 'y', axis=0, tiled=True)  23.4 us
    all_to_all x2, starting transfers between devices, exchange(): return lax.all_to_all(value, axis, split_axis=0, concat_axis=0, tiled=True)  19.2 us
    all_gather x1, blocking collectives, per_device(): pair = lax.all_gather(message, 'c', axis=0, tiled=True)  15.9 us
    all_gather x1, blocking collectives, per_device(): crossed = lax.all_gather(theirs, 'c', axis=0, tiled=False)  13.6 us
    ppermute x8, waiting for transfers between devices, along(): lax.ppermute(value, 'y', [(i, (i + step) % size) for i in range(size)])  7.67 us
  transfers between devices with their start and end apart: 10, of which 7 were waited for; matrix products, arithmetic and copies ran while one was open for 2% of the time, Pallas kernels for 0%

profile of v2, /device:TPU:1, one launch (start us, length us, event | category | flops | bytes accessed | tf_op | source)
XLA Modules:
  0.0 166.0 jit_solution(18326473037793351420)
XLA Ops:
  0.0 1.8 %shard_map.73 = bf16[32,640]{1,0:T(8,128)(2,1)} custom-call(bf16[32,512]{1,0:T(8,128)(2,1)} %tokens_ref.1, s32[4,32]{1,0:T(4,128)} %bitcast.97, s32[8,32]{1,0:T(8,128)} %bitcast.95, f32[8,32]{1,0:T(8,128)} %bitcast.96), custom_call_target="tpu_custom_call" | custom-call | tf_op jit(solution)/shard_map/pallas_call | solution.py:34
  1.8 15.9 %all_gather.10 = bf16[64,640]{1,0:T(8,128)(2,1)S(1)} all-gather(bf16[32,640]{1,0:T(8,128)(2,1)} %shard_map.73), channel_id=1, replica_groups=mesh['x'=4,'z'=16,'c'=2,'y'=8] {'c'}, dimensions={0}, use_global_device_ids=true | all-gather | bytes 122880 | tf_op jit(solution)/shard_map/all_gather | solution.py:101
  18.4 1.2 fusion.1
  19.5 9.3 %all-to-all-start = ((bf16[64,8,512]{2,1,0:T(8,128)(2,1)}), bf16[64,8,512]{2,1,0:T(8,128)(2,1)S(1)}, u32[]{:S(2)}, u32[]{:S(2)}) async-start(bf16[64,8,512]{2,1,0:T(8,128)(2,1)} %fusion.1), calls=%async_computation | async-start | bytes 1048576 | tf_op jit(solution)/shard_map/all_to_all | solution.py:46
  29.2 1.0 slice.95
  30.3 28.3 %all-to-all-done = bf16[64,8,512]{2,1,0:T(8,128)(2,1)S(1)} async-done(((bf16[64,8,512]{2,1,0:T(8,128)(2,1)}), bf16[64,8,512]{2,1,0:T(8,128)(2,1)S(1)}, u32[]{:S(2)}, u32[]{:S(2)}) %all-to-all-start) | async-done | bytes 524320 | tf_op jit(solution)/shard_map/all_to_all | solution.py:46
  58.9 0.7 convolution_convert_fusion
  61.0 3.2 %collective-permute-start = (bf16[64,1152]{1,0:T(8,128)(2,1)S(1)}, bf16[64,1152]{1,0:T(8,128)(2,1)S(1)}, u32[]{:S(2)}, u32[]{:S(2)}) collective-permute-start(bf16[64,1152]{1,0:T(8,128)(2,1)S(1)} %get-tuple-element.22), channel_id=1, source_target_pairs={{0,1},{1,2},{2,3},{3,4},{4,5},{5,6},{6,7},{7,0},{8,9},{9,10},{10,1... | collective-permute-start | bytes 442376 | tf_op jit(solution)/shard_map/ppermute | solution.py:42
  64.3 3.8 %collective-permute-start.4 = (bf16[64,1152]{1,0:T(8,128)(2,1)S(1)}, bf16[64,1152]{1,0:T(8,128)(2,1)S(1)}, u32[]{:S(2)}, u32[]{:S(2)}) collective-permute-start(bf16[64,1152]{1,0:T(8,128)(2,1)S(1)} %get-tuple-element.21), channel_id=1, source_target_pairs={{0,7},{1,0},{2,1},{3,2},{4,3},{5,4},{6,5},{7,6},{8,15},{9,8},{10,9... | collective-permute-start | bytes 442376 | tf_op jit(solution)/shard_map/ppermute | solution.py:42
  68.8 1.9 %collective-permute-start.1 = (bf16[64,2176]{1,0:T(8,128)(2,1)S(1)}, bf16[64,2176]{1,0:T(8,128)(2,1)S(1)}, u32[]{:S(2)}, u32[]{:S(2)}) collective-permute-start(bf16[64,2176]{1,0:T(8,128)(2,1)S(1)} %pad_maximum_fusion), channel_id=1, source_target_pairs={{0,1},{1,2},{2,3},{3,4},{4,5},{5,6},{6,7},{7,0},{8,9},{9,10},{10,1... | collective-permute-start | bytes 835592 | tf_op jit(solution)/shard_map/ppermute | solution.py:42
  70.8 4.6 %collective-permute-start.5 = (bf16[64,2176]{1,0:T(8,128)(2,1)S(1)}, bf16[64,2176]{1,0:T(8,128)(2,1)S(1)}, u32[]{:S(2)}, u32[]{:S(2)}) collective-permute-start(bf16[64,2176]{1,0:T(8,128)(2,1)S(1)} %pad_maximum_fusion.3), channel_id=1, source_target_pairs={{0,7},{1,0},{2,1},{3,2},{4,3},{5,4},{6,5},{7,6},{8,15},{9,8},{10,9... | collective-permute-start | bytes 835592 | tf_op jit(solution)/shard_map/ppermute | solution.py:42
  75.4 1.9 %collective-permute-done.1 = bf16[64,2176]{1,0:T(8,128)(2,1)S(1)} collective-permute-done((bf16[64,2176]{1,0:T(8,128)(2,1)S(1)}, bf16[64,2176]{1,0:T(8,128)(2,1)S(1)}, u32[]{:S(2)}, u32[]{:S(2)}) %collective-permute-start.1) | collective-permute-done | bytes 278560 | tf_op jit(solution)/shard_map/ppermute | solution.py:42
  77.4 1.9 %collective-permute-start.2 = (bf16[64,2176]{1,0:T(8,128)(2,1)S(1)}, bf16[64,2176]{1,0:T(8,128)(2,1)S(1)}, u32[]{:S(2)}, u32[]{:S(2)}) collective-permute-start(bf16[64,2176]{1,0:T(8,128)(2,1)S(1)} %pad_maximum_fusion.1), channel_id=1, source_target_pairs={{0,1},{1,2},{2,3},{3,4},{4,5},{5,6},{6,7},{7,0},{8,9},{9,10},{10,1... | collective-permute-start | bytes 835592 | tf_op jit(solution)/shard_map/ppermute | solution.py:42
  79.4 4.6 %collective-permute-start.6 = (bf16[64,2176]{1,0:T(8,128)(2,1)S(1)}, bf16[64,2176]{1,0:T(8,128)(2,1)S(1)}, u32[]{:S(2)}, u32[]{:S(2)}) collective-permute-start(bf16[64,2176]{1,0:T(8,128)(2,1)S(1)} %pad_maximum_fusion.4), channel_id=1, source_target_pairs={{0,7},{1,0},{2,1},{3,2},{4,3},{5,4},{6,5},{7,6},{8,15},{9,8},{10,9... | collective-permute-start | bytes 835592 | tf_op jit(solution)/shard_map/ppermute | solution.py:42
  84.0 1.9 %collective-permute-done.2 = bf16[64,2176]{1,0:T(8,128)(2,1)S(1)} collective-permute-done((bf16[64,2176]{1,0:T(8,128)(2,1)S(1)}, bf16[64,2176]{1,0:T(8,128)(2,1)S(1)}, u32[]{:S(2)}, u32[]{:S(2)}) %collective-permute-start.2) | collective-permute-done | bytes 278560 | tf_op jit(solution)/shard_map/ppermute | solution.py:42
  86.0 1.9 %collective-permute-start.3 = (bf16[64,2176]{1,0:T(8,128)(2,1)S(1)}, bf16[64,2176]{1,0:T(8,128)(2,1)S(1)}, u32[]{:S(2)}, u32[]{:S(2)}) collective-permute-start(bf16[64,2176]{1,0:T(8,128)(2,1)S(1)} %pad_maximum_fusion.2), channel_id=1, source_target_pairs={{0,1},{1,2},{2,3},{3,4},{4,5},{5,6},{6,7},{7,0},{8,9},{9,10},{10,1... | collective-permute-start | bytes 835592 | tf_op jit(solution)/shard_map/ppermute | solution.py:42
  88.0 4.6 %collective-permute-start.7 = (bf16[64,2048]{1,0:T(8,128)(2,1)S(1)}, bf16[64,2048]{1,0:T(8,128)(2,1)S(1)}, u32[]{:S(2)}, u32[]{:S(2)}) collective-permute-start(bf16[64,2048]{1,0:T(8,128)(2,1)S(1)} %add_convert_fusion), channel_id=1, source_target_pairs={{0,7},{1,0},{2,1},{3,2},{4,3},{5,4},{6,5},{7,6},{8,15},{9,8},{10,9... | collective-permute-start | bytes 786440 | tf_op jit(solution)/shard_map/ppermute | solution.py:42
  92.6 1.9 %collective-permute-done.3 = bf16[64,2176]{1,0:T(8,128)(2,1)S(1)} collective-permute-done((bf16[64,2176]{1,0:T(8,128)(2,1)S(1)}, bf16[64,2176]{1,0:T(8,128)(2,1)S(1)}, u32[]{:S(2)}, u32[]{:S(2)}) %collective-permute-start.3) | collective-permute-done | bytes 278560 | tf_op jit(solution)/shard_map/ppermute | solution.py:42
  94.7 1.4 collective-permute-done.7
  96.3 23.4 %all_gather.11 = bf16[512,1016]{1,0:T(8,128)(2,1)S(1)} all-gather(bf16[64,1016]{1,0:T(8,128)(2,1)S(1)} %fusion.15), channel_id=1, replica_groups=mesh['x'=4,'z'=16,'c'=2,'y'=8] {'y'}, dimensions={0}, use_global_device_ids=true | all-gather | bytes 1170432 | tf_op jit(solution)/shard_map/all_gather | solution.py:136
  119.7 1.5 fusion
  121.2 9.9 %all-to-all-start.1 = ((bf16[64,8,512]{2,1,0:T(8,128)(2,1)}), bf16[64,8,512]{2,1,0:T(8,128)(2,1)S(1)}, u32[]{:S(2)}, u32[]{:S(2)}) async-start(bf16[64,8,512]{2,1,0:T(8,128)(2,1)} %fusion), calls=%async_computation.1 | async-start | bytes 1048576 | tf_op jit(solution)/shard_map/all_to_all | solution.py:46
  131.7 19.7 %all-to-all-done.1 = bf16[64,8,512]{2,1,0:T(8,128)(2,1)S(1)} async-done(((bf16[64,8,512]{2,1,0:T(8,128)(2,1)}), bf16[64,8,512]{2,1,0:T(8,128)(2,1)S(1)}, u32[]{:S(2)}, u32[]{:S(2)}) %all-to-all-start.1) | async-done | bytes 524320 | tf_op jit(solution)/shard_map/all_to_all | solution.py:46
  151.7 13.6 %all_gather.12 = bf16[2,32,512]{2,1,0:T(8,128)(2,1)S(1)} all-gather(bf16[1,32,512]{2,1,0:T(8,128)(2,1)S(1)} %dynamic-slice_convert_fusion), channel_id=1, replica_groups=mesh['x'=4,'z'=16,'c'=2,'y'=8] {'c'}, dimensions={0}, use_global_device_ids=true | all-gather | bytes 98304 | tf_op jit(solution)/shard_map/all_gather | solution.py:148
  (58 shorter events, 5.5 us)
Async XLA Ops:
  0.0 119.7 %copy-start = (bf16[1,1024,512]{2,1,0:T(8,128)(2,1)S(1)}, bf16[1,1024,512]{2,1,0:T(8,128)(2,1)}, u32[]{:S(2)}) copy-start(bf16[1,1024,512]{2,1,0:T(8,128)(2,1)} %param.13) | copy-start | bytes 3145732
  18.2 10.8 %copy-start.1 = (bf16[1,512,1024]{2,1,0:T(8,128)(2,1)S(1)}, bf16[1,512,1024]{2,1,0:T(8,128)(2,1)}, u32[]{:S(2)}) copy-start(bf16[1,512,1024]{2,1,0:T(8,128)(2,1)} %param.12) | copy-start | bytes 3145732
  19.5 39.1 %all-to-all-start = ((bf16[64,8,512]{2,1,0:T(8,128)(2,1)}), bf16[64,8,512]{2,1,0:T(8,128)(2,1)S(1)}, u32[]{:S(2)}, u32[]{:S(2)}) async-start(bf16[64,8,512]{2,1,0:T(8,128)(2,1)} %fusion.1), calls=%async_computation | async-start | bytes 1048576 | tf_op jit(solution)/shard_map/all_to_all | solution.py:46
  58.8 1.2 copy-start.2
  61.0 7.6 %collective-permute-start = (bf16[64,1152]{1,0:T(8,128)(2,1)S(1)}, bf16[64,1152]{1,0:T(8,128)(2,1)S(1)}, u32[]{:S(2)}, u32[]{:S(2)}) collective-permute-start(bf16[64,1152]{1,0:T(8,128)(2,1)S(1)} %get-tuple-element.22), channel_id=1, source_target_pairs={{0,1},{1,2},{2,3},{3,4},{4,5},{5,6},{6,7},{7,0},{8,9},{9,10},{10,1... | collective-permute-start | bytes 442376 | tf_op jit(solution)/shard_map/ppermute | solution.py:42
  64.3 6.4 %collective-permute-start.4 = (bf16[64,1152]{1,0:T(8,128)(2,1)S(1)}, bf16[64,1152]{1,0:T(8,128)(2,1)S(1)}, u32[]{:S(2)}, u32[]{:S(2)}) collective-permute-start(bf16[64,1152]{1,0:T(8,128)(2,1)S(1)} %get-tuple-element.21), channel_id=1, source_target_pairs={{0,7},{1,0},{2,1},{3,2},{4,3},{5,4},{6,5},{7,6},{8,15},{9,8},{10,9... | collective-permute-start | bytes 442376 | tf_op jit(solution)/shard_map/ppermute | solution.py:42
  68.8 8.5 %collective-permute-start.1 = (bf16[64,2176]{1,0:T(8,128)(2,1)S(1)}, bf16[64,2176]{1,0:T(8,128)(2,1)S(1)}, u32[]{:S(2)}, u32[]{:S(2)}) collective-permute-start(bf16[64,2176]{1,0:T(8,128)(2,1)S(1)} %pad_maximum_fusion), channel_id=1, source_target_pairs={{0,1},{1,2},{2,3},{3,4},{4,5},{5,6},{6,7},{7,0},{8,9},{9,10},{10,1... | collective-permute-start | bytes 835592 | tf_op jit(solution)/shard_map/ppermute | solution.py:42
  70.8 8.5 %collective-permute-start.5 = (bf16[64,2176]{1,0:T(8,128)(2,1)S(1)}, bf16[64,2176]{1,0:T(8,128)(2,1)S(1)}, u32[]{:S(2)}, u32[]{:S(2)}) collective-permute-start(bf16[64,2176]{1,0:T(8,128)(2,1)S(1)} %pad_maximum_fusion.3), channel_id=1, source_target_pairs={{0,7},{1,0},{2,1},{3,2},{4,3},{5,4},{6,5},{7,6},{8,15},{9,8},{10,9... | collective-permute-start | bytes 835592 | tf_op jit(solution)/shard_map/ppermute | solution.py:42
  77.4 8.5 %collective-permute-start.2 = (bf16[64,2176]{1,0:T(8,128)(2,1)S(1)}, bf16[64,2176]{1,0:T(8,128)(2,1)S(1)}, u32[]{:S(2)}, u32[]{:S(2)}) collective-permute-start(bf16[64,2176]{1,0:T(8,128)(2,1)S(1)} %pad_maximum_fusion.1), channel_id=1, source_target_pairs={{0,1},{1,2},{2,3},{3,4},{4,5},{5,6},{6,7},{7,0},{8,9},{9,10},{10,1... | collective-permute-start | bytes 835592 | tf_op jit(solution)/shard_map/ppermute | solution.py:42
  79.4 8.5 %collective-permute-start.6 = (bf16[64,2176]{1,0:T(8,128)(2,1)S(1)}, bf16[64,2176]{1,0:T(8,128)(2,1)S(1)}, u32[]{:S(2)}, u32[]{:S(2)}) collective-permute-start(bf16[64,2176]{1,0:T(8,128)(2,1)S(1)} %pad_maximum_fusion.4), channel_id=1, source_target_pairs={{0,7},{1,0},{2,1},{3,2},{4,3},{5,4},{6,5},{7,6},{8,15},{9,8},{10,9... | collective-permute-start | bytes 835592 | tf_op jit(solution)/shard_map/ppermute | solution.py:42
  86.0 8.5 %collective-permute-start.3 = (bf16[64,2176]{1,0:T(8,128)(2,1)S(1)}, bf16[64,2176]{1,0:T(8,128)(2,1)S(1)}, u32[]{:S(2)}, u32[]{:S(2)}) collective-permute-start(bf16[64,2176]{1,0:T(8,128)(2,1)S(1)} %pad_maximum_fusion.2), channel_id=1, source_target_pairs={{0,1},{1,2},{2,3},{3,4},{4,5},{5,6},{6,7},{7,0},{8,9},{9,10},{10,1... | collective-permute-start | bytes 835592 | tf_op jit(solution)/shard_map/ppermute | solution.py:42
  88.0 8.1 %collective-permute-start.7 = (bf16[64,2048]{1,0:T(8,128)(2,1)S(1)}, bf16[64,2048]{1,0:T(8,128)(2,1)S(1)}, u32[]{:S(2)}, u32[]{:S(2)}) collective-permute-start(bf16[64,2048]{1,0:T(8,128)(2,1)S(1)} %add_convert_fusion), channel_id=1, source_target_pairs={{0,7},{1,0},{2,1},{3,2},{4,3},{5,4},{6,5},{7,6},{8,15},{9,8},{10,9... | collective-permute-start | bytes 786440 | tf_op jit(solution)/shard_map/ppermute | solution.py:42
  121.2 30.3 %all-to-all-start.1 = ((bf16[64,8,512]{2,1,0:T(8,128)(2,1)}), bf16[64,8,512]{2,1,0:T(8,128)(2,1)S(1)}, u32[]{:S(2)}, u32[]{:S(2)}) async-start(bf16[64,8,512]{2,1,0:T(8,128)(2,1)} %fusion), calls=%async_computation.1 | async-start | bytes 1048576 | tf_op jit(solution)/shard_map/all_to_all | solution.py:46

commit v3 on v2

--- a/solution.py
+++ b/solution.py
@@ -1,3 +1,5 @@
+import functools
+
 import jax
 import jax.numpy as jnp
 from jax import lax
@@ -11,7 +13,7 @@
 CHIPS = ("x", "z")
 
 
-def message_kernel(tokens_ref, exp_ref, routes_ref, scores_ref, out_ref):
+def message_kernel(n_experts, tokens_ref, exp_ref, routes_ref, scores_ref, out_ref):
     tok, feat = tokens_ref.shape
     topk, blocks = routes_ref.shape[0], exp_ref.shape[0]
     factor = (1 << (exp_ref[...] + 16)).astype(F32) * (1.0 / 65536.0)
@@ -26,14 +28,30 @@
         part = slice(i * LANES, (i + 1) * LANES)
         scale = columns[:, 2 * topk + i : 2 * topk + i + 1]
         out_ref[:, part] = (tokens_ref[:, part].astype(F32) * scale).astype(BF)
-    out_ref[:, feat:] = columns.astype(BF)
+    lane = lax.broadcasted_iota(jnp.int32, (tok, 2 * LANES), 1)
+    peer, core = lane % LANES, lane // LANES
+    expert = jnp.where(peer < n_experts // 2, peer * 2 + core, -1).astype(F32)
+    named = jnp.zeros((tok, 2 * LANES), F32)
+    weight = jnp.zeros((tok, 2 * LANES), F32)
+    for k in range(topk):
+        hit = columns[:, k : k + 1] == expert
+        named = jnp.where(hit, 1.0, named)
+        weight = jnp.where(hit, columns[:, topk + k : topk + k + 1], weight)
+    order = lax.broadcasted_iota(jnp.int32, (tok, tok), 0) > lax.broadcasted_iota(jnp.int32, (tok, tok), 1)
+    before = jnp.dot(order.astype(BF), named.astype(BF), preferred_element_type=F32)
+    slot = jnp.where(named > 0.0, before, -1.0)
+    for c in range(2):
+        part = slice(c * LANES, (c + 1) * LANES)
+        at = feat + 2 * c * LANES
+        out_ref[:, at : at + LANES] = slot[:, part].astype(BF)
+        out_ref[:, at + LANES : at + 2 * LANES] = weight[:, part].astype(BF)
 
 
-def make_message(tokens_q, scale_exp, routes, route_scores):
+def make_message(tokens_q, scale_exp, routes, route_scores, n_experts):
     tok, feat = tokens_q.shape
     return pl.pallas_call(
-        message_kernel,
-        out_shape=jax.ShapeDtypeStruct((tok, feat + LANES), BF),
+        functools.partial(message_kernel, n_experts),
+        out_shape=jax.ShapeDtypeStruct((tok, feat + 4 * LANES), BF),
     )(tokens_q, scale_exp.T, routes.T, route_scores.T)
 
 
@@ -89,7 +107,6 @@
 def per_device(tokens_q, scale_exp, routes, route_scores, w_gate, w_up, w_down):
     n_c, n_y, peers = lax.axis_size("c"), lax.axis_size("y"), lax.axis_size(CHIPS)
     tok, feat = tokens_q.shape
-    topk = routes.shape[1]
     hid = w_gate.shape[2]
     tail_cols = LANES // (2 * n_y)
     core = lax.axis_index("c")
@@ -97,18 +114,13 @@
     slots = n_c * CAP
     total_rows = peers * slots
 
-    message = make_message(tokens_q, scale_exp, routes, route_scores)
+    message = make_message(tokens_q, scale_exp, routes, route_scores, peers * n_c)
     pair = lax.all_gather(message, "c", axis=0, tiled=True)
-    pair_routes = pair[:, feat : feat + topk].astype(jnp.int32)
-    pair_mix = pair[:, feat + topk : feat + 2 * topk].astype(F32)
-
-    expert = jnp.arange(peers, dtype=jnp.int32) * n_c + core
-    picked = pair_routes[:, :, None] == expert[None, None, :]
-    weight = jnp.sum(jnp.where(picked, pair_mix[:, :, None], 0.0), axis=1)
-    named = jnp.any(picked, axis=1).astype(jnp.int32).reshape(n_c, tok, peers)
-    before = jnp.cumsum(named, axis=1, dtype=jnp.int32) - named
-    block = jnp.arange(n_c, dtype=jnp.int32)[:, None, None]
-    slot = jnp.where(named > 0, block * CAP + before, -1).reshape(n_c * tok, peers)
+    mine = lax.dynamic_slice_in_dim(pair, feat + core * 2 * LANES, 2 * LANES, 1)
+    weight = mine[:, LANES : LANES + peers].astype(F32)
+    block = jnp.arange(n_c * tok, dtype=jnp.int32)[:, None] // tok
+    slot = mine[:, :peers].astype(jnp.int32)
+    slot = jnp.where(slot >= 0, block * CAP + slot, -1)
     slot_ids = jnp.arange(slots, dtype=jnp.int32)
     select = slot.T[:, None, :] == slot_ids[None, :, None]
     select_rows = select.astype(BF).reshape(total_rows, n_c * tok)

time: 167 us -> 166 us (level)
  transfers between devices with their start and end apart: 10 -> 10, of which waited for: 7 -> 7; matrix products, arithmetic and copies ran while one was open for 2% -> 1% of each run, Pallas kernels for 0% -> 0%
where the time goes in v3:
time: 166 us
  waiting for transfers between devices  55.9 us (34%)
  blocking collectives  52.9 us (32%)
  starting transfers between devices  45.8 us (28%)
  matrix products  4.53 us (3%)
  local copies, waits for them, and re-layouts  2.64 us (2%)
  Pallas kernels  1.93 us (1%)
    all_to_all x2, waiting for transfers between devices, exchange(): return lax.all_to_all(value, axis, split_axis=0, concat_axis=0, tiled=True)  48.2 us
    ppermute x8, starting transfers between devices, along(): lax.ppermute(value, 'y', [(i, (i + step) % size) for i in range(size)])  26.5 us
    all_gather x1, blocking collectives, per_device(): hidden_main = lax.all_gather(hidden, 'y', axis=0, tiled=True)  23.4 us
    all_to_all x2, starting transfers between devices, exchange(): return lax.all_to_all(value, axis, split_axis=0, concat_axis=0, tiled=True)  19.3 us
    all_gather x1, blocking collectives, per_device(): pair = lax.all_gather(message, 'c', axis=0, tiled=True)  15.9 us
    all_gather x1, blocking collectives, per_device(): crossed = lax.all_gather(theirs, 'c', axis=0, tiled=False)  13.6 us
    ppermute x8, waiting for transfers between devices, along(): lax.ppermute(value, 'y', [(i, (i + step) % size) for i in range(size)])  7.67 us
  transfers between devices with their start and end apart: 10, of which 7 were waited for; matrix products, arithmetic and copies ran while one was open for 1% of the time, Pallas kernels for 0%

profile of v3, /device:TPU:1, one launch (start us, length us, event | category | flops | bytes accessed | tf_op | source)
XLA Modules:
  0.0 165.7 jit_solution(11907266198883940288)
XLA Ops:
  0.0 1.9 %shard_map.73 = bf16[32,1024]{1,0:T(8,128)(2,1)} custom-call(bf16[32,512]{1,0:T(8,128)(2,1)} %tokens_ref.1, s32[4,32]{1,0:T(4,128)} %bitcast.89, s32[8,32]{1,0:T(8,128)} %bitcast.87, f32[8,32]{1,0:T(8,128)} %bitcast.88), custom_call_target="tpu_custom_call" | custom-call | tf_op jit(solution)/shard_map/pallas_call | solution.py:52
  1.9 15.9 %all_gather.10 = bf16[64,1024]{1,0:T(8,128)(2,1)S(1)} all-gather(bf16[32,1024]{1,0:T(8,128)(2,1)} %shard_map.73), channel_id=1, replica_groups=mesh['x'=4,'z'=16,'c'=2,'y'=8] {'c'}, dimensions={0}, use_global_device_ids=true | all-gather | bytes 196608 | tf_op jit(solution)/shard_map/all_gather | solution.py:118
  18.1 1.2 fusion.1
  19.3 9.3 %all-to-all-start = ((bf16[64,8,512]{2,1,0:T(8,128)(2,1)}), bf16[64,8,512]{2,1,0:T(8,128)(2,1)S(1)}, u32[]{:S(2)}, u32[]{:S(2)}) async-start(bf16[64,8,512]{2,1,0:T(8,128)(2,1)} %fusion.1), calls=%async_computation | async-start | bytes 1048576 | tf_op jit(solution)/shard_map/all_to_all | solution.py:64
  28.9 1.0 slice.95
  30.0 28.3 %all-to-all-done = bf16[64,8,512]{2,1,0:T(8,128)(2,1)S(1)} async-done(((bf16[64,8,512]{2,1,0:T(8,128)(2,1)}), bf16[64,8,512]{2,1,0:T(8,128)(2,1)S(1)}, u32[]{:S(2)}, u32[]{:S(2)}) %all-to-all-start) | async-done | bytes 524320 | tf_op jit(solution)/shard_map/all_to_all | solution.py:64
  58.6 0.7 convolution_convert_fusion
  60.8 3.2 %collective-permute-start = (bf16[64,1152]{1,0:T(8,128)(2,1)S(1)}, bf16[64,1152]{1,0:T(8,128)(2,1)S(1)}, u32[]{:S(2)}, u32[]{:S(2)}) collective-permute-start(bf16[64,1152]{1,0:T(8,128)(2,1)S(1)} %get-tuple-element.20), channel_id=1, source_target_pairs={{0,1},{1,2},{2,3},{3,4},{4,5},{5,6},{6,7},{7,0},{8,9},{9,10},{10,1... | collective-permute-start | bytes 442376 | tf_op jit(solution)/shard_map/ppermute | solution.py:60
  64.0 3.8 %collective-permute-start.4 = (bf16[64,1152]{1,0:T(8,128)(2,1)S(1)}, bf16[64,1152]{1,0:T(8,128)(2,1)S(1)}, u32[]{:S(2)}, u32[]{:S(2)}) collective-permute-start(bf16[64,1152]{1,0:T(8,128)(2,1)S(1)} %get-tuple-element.19), channel_id=1, source_target_pairs={{0,7},{1,0},{2,1},{3,2},{4,3},{5,4},{6,5},{7,6},{8,15},{9,8},{10,9... | collective-permute-start | bytes 442376 | tf_op jit(solution)/shard_map/ppermute | solution.py:60
  68.5 1.9 %collective-permute-start.1 = (bf16[64,2176]{1,0:T(8,128)(2,1)S(1)}, bf16[64,2176]{1,0:T(8,128)(2,1)S(1)}, u32[]{:S(2)}, u32[]{:S(2)}) collective-permute-start(bf16[64,2176]{1,0:T(8,128)(2,1)S(1)} %pad_maximum_fusion), channel_id=1, source_target_pairs={{0,1},{1,2},{2,3},{3,4},{4,5},{5,6},{6,7},{7,0},{8,9},{9,10},{10,1... | collective-permute-start | bytes 835592 | tf_op jit(solution)/shard_map/ppermute | solution.py:60
  70.5 4.6 %collective-permute-start.5 = (bf16[64,2176]{1,0:T(8,128)(2,1)S(1)}, bf16[64,2176]{1,0:T(8,128)(2,1)S(1)}, u32[]{:S(2)}, u32[]{:S(2)}) collective-permute-start(bf16[64,2176]{1,0:T(8,128)(2,1)S(1)} %pad_maximum_fusion.3), channel_id=1, source_target_pairs={{0,7},{1,0},{2,1},{3,2},{4,3},{5,4},{6,5},{7,6},{8,15},{9,8},{10,9... | collective-permute-start | bytes 835592 | tf_op jit(solution)/shard_map/ppermute | solution.py:60
  75.1 1.9 %collective-permute-done.1 = bf16[64,2176]{1,0:T(8,128)(2,1)S(1)} collective-permute-done((bf16[64,2176]{1,0:T(8,128)(2,1)S(1)}, bf16[64,2176]{1,0:T(8,128)(2,1)S(1)}, u32[]{:S(2)}, u32[]{:S(2)}) %collective-permute-start.1) | collective-permute-done | bytes 278560 | tf_op jit(solution)/shard_map/ppermute | solution.py:60
  77.1 1.9 %collective-permute-start.2 = (bf16[64,2176]{1,0:T(8,128)(2,1)S(1)}, bf16[64,2176]{1,0:T(8,128)(2,1)S(1)}, u32[]{:S(2)}, u32[]{:S(2)}) collective-permute-start(bf16[64,2176]{1,0:T(8,128)(2,1)S(1)} %pad_maximum_fusion.1), channel_id=1, source_target_pairs={{0,1},{1,2},{2,3},{3,4},{4,5},{5,6},{6,7},{7,0},{8,9},{9,10},{10,1... | collective-permute-start | bytes 835592 | tf_op jit(solution)/shard_map/ppermute | solution.py:60
  79.1 4.6 %collective-permute-start.6 = (bf16[64,2176]{1,0:T(8,128)(2,1)S(1)}, bf16[64,2176]{1,0:T(8,128)(2,1)S(1)}, u32[]{:S(2)}, u32[]{:S(2)}) collective-permute-start(bf16[64,2176]{1,0:T(8,128)(2,1)S(1)} %pad_maximum_fusion.4), channel_id=1, source_target_pairs={{0,7},{1,0},{2,1},{3,2},{4,3},{5,4},{6,5},{7,6},{8,15},{9,8},{10,9... | collective-permute-start | bytes 835592 | tf_op jit(solution)/shard_map/ppermute | solution.py:60
  83.7 1.9 %collective-permute-done.2 = bf16[64,2176]{1,0:T(8,128)(2,1)S(1)} collective-permute-done((bf16[64,2176]{1,0:T(8,128)(2,1)S(1)}, bf16[64,2176]{1,0:T(8,128)(2,1)S(1)}, u32[]{:S(2)}, u32[]{:S(2)}) %collective-permute-start.2) | collective-permute-done | bytes 278560 | tf_op jit(solution)/shard_map/ppermute | solution.py:60
  85.7 1.9 %collective-permute-start.3 = (bf16[64,2176]{1,0:T(8,128)(2,1)S(1)}, bf16[64,2176]{1,0:T(8,128)(2,1)S(1)}, u32[]{:S(2)}, u32[]{:S(2)}) collective-permute-start(bf16[64,2176]{1,0:T(8,128)(2,1)S(1)} %pad_maximum_fusion.2), channel_id=1, source_target_pairs={{0,1},{1,2},{2,3},{3,4},{4,5},{5,6},{6,7},{7,0},{8,9},{9,10},{10,1... | collective-permute-start | bytes 835592 | tf_op jit(solution)/shard_map/ppermute | solution.py:60
  87.7 4.6 %collective-permute-start.7 = (bf16[64,2048]{1,0:T(8,128)(2,1)S(1)}, bf16[64,2048]{1,0:T(8,128)(2,1)S(1)}, u32[]{:S(2)}, u32[]{:S(2)}) collective-permute-start(bf16[64,2048]{1,0:T(8,128)(2,1)S(1)} %add_convert_fusion), channel_id=1, source_target_pairs={{0,7},{1,0},{2,1},{3,2},{4,3},{5,4},{6,5},{7,6},{8,15},{9,8},{10,9... | collective-permute-start | bytes 786440 | tf_op jit(solution)/shard_map/ppermute | solution.py:60
  92.3 1.9 %collective-permute-done.3 = bf16[64,2176]{1,0:T(8,128)(2,1)S(1)} collective-permute-done((bf16[64,2176]{1,0:T(8,128)(2,1)S(1)}, bf16[64,2176]{1,0:T(8,128)(2,1)S(1)}, u32[]{:S(2)}, u32[]{:S(2)}) %collective-permute-start.3) | collective-permute-done | bytes 278560 | tf_op jit(solution)/shard_map/ppermute | solution.py:60
  94.4 1.4 collective-permute-done.7
  96.0 23.4 %all_gather.11 = bf16[512,1016]{1,0:T(8,128)(2,1)S(1)} all-gather(bf16[64,1016]{1,0:T(8,128)(2,1)S(1)} %fusion.14), channel_id=1, replica_groups=mesh['x'=4,'z'=16,'c'=2,'y'=8] {'y'}, dimensions={0}, use_global_device_ids=true | all-gather | bytes 1170432 | tf_op jit(solution)/shard_map/all_gather | solution.py:148
  119.4 1.5 fusion
  120.9 9.9 %all-to-all-start.1 = ((bf16[64,8,512]{2,1,0:T(8,128)(2,1)}), bf16[64,8,512]{2,1,0:T(8,128)(2,1)S(1)}, u32[]{:S(2)}, u32[]{:S(2)}) async-start(bf16[64,8,512]{2,1,0:T(8,128)(2,1)} %fusion), calls=%async_computation.1 | async-start | bytes 1048576 | tf_op jit(solution)/shard_map/all_to_all | solution.py:64
  131.3 19.9 %all-to-all-done.1 = bf16[64,8,512]{2,1,0:T(8,128)(2,1)S(1)} async-done(((bf16[64,8,512]{2,1,0:T(8,128)(2,1)}), bf16[64,8,512]{2,1,0:T(8,128)(2,1)S(1)}, u32[]{:S(2)}, u32[]{:S(2)}) %all-to-all-start.1) | async-done | bytes 524320 | tf_op jit(solution)/shard_map/all_to_all | solution.py:64
  151.4 13.6 %all_gather.12 = bf16[2,32,512]{2,1,0:T(8,128)(2,1)S(1)} all-gather(bf16[1,32,512]{2,1,0:T(8,128)(2,1)S(1)} %dynamic-slice_convert_fusion), channel_id=1, replica_groups=mesh['x'=4,'z'=16,'c'=2,'y'=8] {'c'}, dimensions={0}, use_global_device_ids=true | all-gather | bytes 98304 | tf_op jit(solution)/shard_map/all_gather | solution.py:160
  (51 shorter events, 4.9 us)
Async XLA Ops:
  0.0 119.4 %copy-start = (bf16[1,1024,512]{2,1,0:T(8,128)(2,1)S(1)}, bf16[1,1024,512]{2,1,0:T(8,128)(2,1)}, u32[]{:S(2)}) copy-start(bf16[1,1024,512]{2,1,0:T(8,128)(2,1)} %param.13) | copy-start | bytes 3145732
  17.8 10.9 %copy-start.1 = (bf16[1,512,1024]{2,1,0:T(8,128)(2,1)S(1)}, bf16[1,512,1024]{2,1,0:T(8,128)(2,1)}, u32[]{:S(2)}) copy-start(bf16[1,512,1024]{2,1,0:T(8,128)(2,1)} %param.12) | copy-start | bytes 3145732
  19.3 39.1 %all-to-all-start = ((bf16[64,8,512]{2,1,0:T(8,128)(2,1)}), bf16[64,8,512]{2,1,0:T(8,128)(2,1)S(1)}, u32[]{:S(2)}, u32[]{:S(2)}) async-start(bf16[64,8,512]{2,1,0:T(8,128)(2,1)} %fusion.1), calls=%async_computation | async-start | bytes 1048576 | tf_op jit(solution)/shard_map/all_to_all | solution.py:64
  58.6 1.2 copy-start.2
  60.8 7.6 %collective-permute-start = (bf16[64,1152]{1,0:T(8,128)(2,1)S(1)}, bf16[64,1152]{1,0:T(8,128)(2,1)S(1)}, u32[]{:S(2)}, u32[]{:S(2)}) collective-permute-start(bf16[64,1152]{1,0:T(8,128)(2,1)S(1)} %get-tuple-element.20), channel_id=1, source_target_pairs={{0,1},{1,2},{2,3},{3,4},{4,5},{5,6},{6,7},{7,0},{8,9},{9,10},{10,1... | collective-permute-start | bytes 442376 | tf_op jit(solution)/shard_map/ppermute | solution.py:60
  64.0 6.4 %collective-permute-start.4 = (bf16[64,1152]{1,0:T(8,128)(2,1)S(1)}, bf16[64,1152]{1,0:T(8,128)(2,1)S(1)}, u32[]{:S(2)}, u32[]{:S(2)}) collective-permute-start(bf16[64,1152]{1,0:T(8,128)(2,1)S(1)} %get-tuple-element.19), channel_id=1, source_target_pairs={{0,7},{1,0},{2,1},{3,2},{4,3},{5,4},{6,5},{7,6},{8,15},{9,8},{10,9... | collective-permute-start | bytes 442376 | tf_op jit(solution)/shard_map/ppermute | solution.py:60
  68.5 8.5 %collective-permute-start.1 = (bf16[64,2176]{1,0:T(8,128)(2,1)S(1)}, bf16[64,2176]{1,0:T(8,128)(2,1)S(1)}, u32[]{:S(2)}, u32[]{:S(2)}) collective-permute-start(bf16[64,2176]{1,0:T(8,128)(2,1)S(1)} %pad_maximum_fusion), channel_id=1, source_target_pairs={{0,1},{1,2},{2,3},{3,4},{4,5},{5,6},{6,7},{7,0},{8,9},{9,10},{10,1... | collective-permute-start | bytes 835592 | tf_op jit(solution)/shard_map/ppermute | solution.py:60
  70.5 8.5 %collective-permute-start.5 = (bf16[64,2176]{1,0:T(8,128)(2,1)S(1)}, bf16[64,2176]{1,0:T(8,128)(2,1)S(1)}, u32[]{:S(2)}, u32[]{:S(2)}) collective-permute-start(bf16[64,2176]{1,0:T(8,128)(2,1)S(1)} %pad_maximum_fusion.3), channel_id=1, source_target_pairs={{0,7},{1,0},{2,1},{3,2},{4,3},{5,4},{6,5},{7,6},{8,15},{9,8},{10,9... | collective-permute-start | bytes 835592 | tf_op jit(solution)/shard_map/ppermute | solution.py:60
  77.1 8.5 %collective-permute-start.2 = (bf16[64,2176]{1,0:T(8,128)(2,1)S(1)}, bf16[64,2176]{1,0:T(8,128)(2,1)S(1)}, u32[]{:S(2)}, u32[]{:S(2)}) collective-permute-start(bf16[64,2176]{1,0:T(8,128)(2,1)S(1)} %pad_maximum_fusion.1), channel_id=1, source_target_pairs={{0,1},{1,2},{2,3},{3,4},{4,5},{5,6},{6,7},{7,0},{8,9},{9,10},{10,1... | collective-permute-start | bytes 835592 | tf_op jit(solution)/shard_map/ppermute | solution.py:60
  79.1 8.5 %collective-permute-start.6 = (bf16[64,2176]{1,0:T(8,128)(2,1)S(1)}, bf16[64,2176]{1,0:T(8,128)(2,1)S(1)}, u32[]{:S(2)}, u32[]{:S(2)}) collective-permute-start(bf16[64,2176]{1,0:T(8,128)(2,1)S(1)} %pad_maximum_fusion.4), channel_id=1, source_target_pairs={{0,7},{1,0},{2,1},{3,2},{4,3},{5,4},{6,5},{7,6},{8,15},{9,8},{10,9... | collective-permute-start | bytes 835592 | tf_op jit(solution)/shard_map/ppermute | solution.py:60
  85.7 8.5 %collective-permute-start.3 = (bf16[64,2176]{1,0:T(8,128)(2,1)S(1)}, bf16[64,2176]{1,0:T(8,128)(2,1)S(1)}, u32[]{:S(2)}, u32[]{:S(2)}) collective-permute-start(bf16[64,2176]{1,0:T(8,128)(2,1)S(1)} %pad_maximum_fusion.2), channel_id=1, source_target_pairs={{0,1},{1,2},{2,3},{3,4},{4,5},{5,6},{6,7},{7,0},{8,9},{9,10},{10,1... | collective-permute-start | bytes 835592 | tf_op jit(solution)/shard_map/ppermute | solution.py:60
  87.7 8.1 %collective-permute-start.7 = (bf16[64,2048]{1,0:T(8,128)(2,1)S(1)}, bf16[64,2048]{1,0:T(8,128)(2,1)S(1)}, u32[]{:S(2)}, u32[]{:S(2)}) collective-permute-start(bf16[64,2048]{1,0:T(8,128)(2,1)S(1)} %add_convert_fusion), channel_id=1, source_target_pairs={{0,7},{1,0},{2,1},{3,2},{4,3},{5,4},{6,5},{7,6},{8,15},{9,8},{10,9... | collective-permute-start | bytes 786440 | tf_op jit(solution)/shard_map/ppermute | solution.py:60
  120.9 30.3 %all-to-all-start.1 = ((bf16[64,8,512]{2,1,0:T(8,128)(2,1)}), bf16[64,8,512]{2,1,0:T(8,128)(2,1)S(1)}, u32[]{:S(2)}, u32[]{:S(2)}) async-start(bf16[64,8,512]{2,1,0:T(8,128)(2,1)} %fusion), calls=%async_computation.1 | async-start | bytes 1048576 | tf_op jit(solution)/shard_map/all_to_all | solution.py:64
